TPU v7x, 512 devices: a whole 4x4x16 slice. The times are simulated.
512 devices in a mesh: section: 16 (over x, z_lo), seq: 16 (over z_hi, y), cfg: 2 (over core).
Axes of the slice: x: 4, y: 4, z: 16 (z_hi: 4, z_lo: 4; z = z_hi * 4 + z_lo), core: 2. Of those that a mesh axis runs over, the one named last changes fastest.
Arguments:
- latent: bfloat16 [64, 3072], P(None, 'seq'), may hold values from -6 to 6
- timestep: int32 [1], replicated, may hold values from 0 to 7
- modulation: bfloat16 [16, 16, 3, 3072], P('section', 'cfg'), parts along dimension 1, may hold values from -4 to 4
- qkv_weight: bfloat16 [16, 3072, 3, 2048], P('section', None, None, 'seq'), may hold values from -0.109375 to 0.109375
- out_weight: bfloat16 [16, 2048, 3072], P('section', None, 'seq'), may hold values from -0.125 to 0.125
- stale_kv: bfloat16 [16, 2, 128, 2048], P('section', None, 'cfg', 'seq'), parts along dimension 2, may hold values from -6 to 6
Outputs:
- hidden_out: bfloat16 [16, 128, 3072], P('section', 'cfg', 'seq'), parts along dimension 1
- kv_next: bfloat16 [16, 2, 128, 2048], P('section', None, 'cfg', 'seq'), parts along dimension 2
There are 2 independent parts, one for each index of `cfg`. A program takes and returns all parts, laid end to end along the dimension named above; an argument that names none is the same for every part. Nothing has to cross between parts.
All inputs are finite; a program needn't handle non-finite values.
Results may differ from a plain program's by a relative error of at most 0.02.
Values may be sent and summed in bfloat16 or wider, within the bound.
A program may use at most 64 MiB of HBM per device.

v0:
```python
import jax
import jax.numpy as jnp
from jax import lax
from jax.sharding import PartitionSpec as P

D = 3072
HEAD_DIM = 128
PATCHES = 2
PATCH_TOK = 32
TOKENS = 64


EPS_NORM = 1e-06


def passed_along(block, axis, distance):
    devices = range(lax.axis_size(axis))
    route = [(i - distance, i) for i in devices if i - distance in devices]
    return lax.ppermute(block, axis, route)


def norm_rows(values):
    center = jnp.mean(values, axis=-1, keepdims=True)
    centred = values - center
    spread = jnp.mean(centred * centred, axis=-1, keepdims=True)
    return centred / jnp.sqrt(spread + EPS_NORM)


def rms_heads(values):
    return values / jnp.sqrt(jnp.mean(values * values, axis=-1, keepdims=True) + EPS_NORM)


def on_device(latent, timestep, modulation, qkv_weight, out_weight, stale_kv):
    section_count = lax.axis_size("section")
    section_pos = lax.axis_index("section")
    member = lax.axis_index("seq")
    width_part = latent.shape[1]
    inner_part = qkv_weight.shape[3]
    heads_part = inner_part // HEAD_DIM
    mod_table = lax.dynamic_index_in_dim(modulation[0], timestep[0], 0, keepdims=False).astype(
        jnp.float32
    )
    shift_vec = mod_table[0]
    scale_vec = mod_table[1]
    gate_part = lax.dynamic_slice_in_dim(mod_table[2], member * width_part, width_part, 0)
    joint_weight = qkv_weight[0].reshape(D, 3 * inner_part)
    projection = out_weight[0]
    tick_count = PATCHES + section_count - 1

    def attend(whole_rows, key_cache, value_cache, row_start):
        normed = (norm_rows(whole_rows.astype(jnp.float32)) * (1.0 + scale_vec) + shift_vec).astype(
            jnp.bfloat16
        )
        projected = jnp.dot(normed, joint_weight, preferred_element_type=jnp.float32)
        projected = projected.reshape(PATCH_TOK, 3, heads_part, HEAD_DIM)
        query_rows = rms_heads(projected[:, 0]).astype(jnp.bfloat16)
        key_rows = rms_heads(projected[:, 1]).astype(jnp.bfloat16).reshape(PATCH_TOK, inner_part)
        value_rows = projected[:, 2].astype(jnp.bfloat16).reshape(PATCH_TOK, inner_part)
        key_cache = lax.dynamic_update_slice_in_dim(key_cache, key_rows, row_start, 0)
        value_cache = lax.dynamic_update_slice_in_dim(value_cache, value_rows, row_start, 0)
        scores = jnp.einsum(
            "phd,thd->hpt",
            query_rows,
            key_cache.reshape(TOKENS, heads_part, HEAD_DIM),
            preferred_element_type=jnp.float32,
        ) * HEAD_DIM ** (-0.5)
        exponent = jnp.exp(scores)
        weights_soft = (exponent / jnp.sum(exponent, axis=-1, keepdims=True)).astype(jnp.bfloat16)
        attended = jnp.einsum(
            "hpt,thd->phd",
            weights_soft,
            value_cache.reshape(TOKENS, heads_part, HEAD_DIM),
            preferred_element_type=jnp.float32,
        )
        return (
            attended.astype(jnp.bfloat16).reshape(PATCH_TOK, inner_part),
            key_cache,
            value_cache,
        )

    def project(slab_part):
        return jnp.dot(slab_part, projection, preferred_element_type=jnp.float32)

    incoming = jnp.zeros((PATCH_TOK, width_part), jnp.bfloat16)

    def run_tick(tick_num, loop_state):
        carried, key_cache, value_cache, stored = loop_state
        patch_num = tick_num - section_pos
        active = (patch_num >= 0) & (patch_num < PATCHES)
        row_start = jnp.clip(patch_num, 0, PATCHES - 1) * PATCH_TOK
        fresh_rows = lax.dynamic_slice_in_dim(latent, row_start, PATCH_TOK, 0)
        patch_rows = jnp.where(section_pos == 0, fresh_rows, carried)
        whole_rows = lax.all_gather(patch_rows, "seq", axis=1, tiled=True)
        attended, new_keys, new_values = attend(whole_rows, key_cache, value_cache, row_start)
        key_cache = jnp.where(active, new_keys, key_cache)
        value_cache = jnp.where(active, new_values, value_cache)
        update = project(lax.all_gather(attended, "seq", axis=1, tiled=True))
        result = (patch_rows.astype(jnp.float32) + gate_part * update).astype(jnp.bfloat16)
        stored = jnp.where(
            active, lax.dynamic_update_slice_in_dim(stored, result, row_start, 0), stored
        )
        outgoing = passed_along(result, "section", 1)
        return (outgoing, key_cache, value_cache, stored)

    initial = (
        incoming,
        stale_kv[0, 0],
        stale_kv[0, 1],
        jnp.zeros((TOKENS, width_part), jnp.bfloat16),
    )
    carried, key_cache, value_cache, stored = lax.fori_loop(0, tick_count, run_tick, initial)
    return (stored[None], jnp.stack([key_cache, value_cache])[None])


def solution(mesh):
    placed = (
        P(None, "seq"),
        P(),
        P("section", "cfg", None, None),
        P("section", None, None, "seq"),
        P("section", None, "seq"),
        P("section", None, "cfg", "seq"),
    )
    return jax.shard_map(
        on_device,
        mesh=mesh,
        in_specs=placed,
        out_specs=(P("section", "cfg", "seq"), P("section", None, "cfg", "seq")),
        check_vma=False,
    )
```

profile of v0, /device:TPU:6, one launch (start us, length us, event | category | flops | bytes accessed | tf_op | source)
XLA Modules:
  0.0 1848.4 jit_solution(17571707418577992777)
XLA Ops:
  9.8 1837.9 %while.20 = (s32[]{:T(128)}, bf16[32,192]{1,0:T(8,128)(2,1)S(1)}, bf16[64,128]{1,0:T(8,128)(2,1)S(1)}, bf16[64,128]{1,0:T(8,128)(2,1)S(1)}, bf16[64,192]{1,0:T(8...) while((s32[]{:T(128)}, bf16[32,192]{1,0:T(8,128)(2,1)S(1)}, ...), condition=%wide.region_6.7_spmd, body=%wide.region_0.6_spmd.sunk | while | flops 102802504 | bytes 7000136 | solution.py:111
  9.9 60.3 %all-gather.4 = bf16[16,192,32]{1,2,0:T(8,128)(2,1)S(1)} all-gather(bf16[1,192,32]{1,2,0:T(8,128)(2,1)S(1)} %fusion.37), channel_id=1, replica_groups=mesh['section'=16,'seq'=16,'cfg'=2] {'seq'}, dimensions={0}, use_global_device_ids=true | all-gather | bytes 208896 | tf_op jit(solution)/shard_map/while/body/eval_jaxpr/all_gather | solution.py:93
  129.1 48.7 %all-gather.4 = bf16[16,192,32]{1,2,0:T(8,128)(2,1)S(1)} all-gather(bf16[1,192,32]{1,2,0:T(8,128)(2,1)S(1)} %fusion.37), channel_id=1, replica_groups=mesh['section'=16,'seq'=16,'cfg'=2] {'seq'}, dimensions={0}, use_global_device_ids=true | all-gather | bytes 208896 | tf_op jit(solution)/shard_map/while/body/eval_jaxpr/all_gather | solution.py:93
  236.8 48.4 %all-gather.4 = bf16[16,192,32]{1,2,0:T(8,128)(2,1)S(1)} all-gather(bf16[1,192,32]{1,2,0:T(8,128)(2,1)S(1)} %fusion.37), channel_id=1, replica_groups=mesh['section'=16,'seq'=16,'cfg'=2] {'seq'}, dimensions={0}, use_global_device_ids=true | all-gather | bytes 208896 | tf_op jit(solution)/shard_map/while/body/eval_jaxpr/all_gather | solution.py:93
  344.7 48.1 %all-gather.4 = bf16[16,192,32]{1,2,0:T(8,128)(2,1)S(1)} all-gather(bf16[1,192,32]{1,2,0:T(8,128)(2,1)S(1)} %fusion.37), channel_id=1, replica_groups=mesh['section'=16,'seq'=16,'cfg'=2] {'seq'}, dimensions={0}, use_global_device_ids=true | all-gather | bytes 208896 | tf_op jit(solution)/shard_map/while/body/eval_jaxpr/all_gather | solution.py:93
  452.0 48.3 %all-gather.4 = bf16[16,192,32]{1,2,0:T(8,128)(2,1)S(1)} all-gather(bf16[1,192,32]{1,2,0:T(8,128)(2,1)S(1)} %fusion.37), channel_id=1, replica_groups=mesh['section'=16,'seq'=16,'cfg'=2] {'seq'}, dimensions={0}, use_global_device_ids=true | all-gather | bytes 208896 | tf_op jit(solution)/shard_map/while/body/eval_jaxpr/all_gather | solution.py:93
  559.3 48.6 %all-gather.4 = bf16[16,192,32]{1,2,0:T(8,128)(2,1)S(1)} all-gather(bf16[1,192,32]{1,2,0:T(8,128)(2,1)S(1)} %fusion.37), channel_id=1, replica_groups=mesh['section'=16,'seq'=16,'cfg'=2] {'seq'}, dimensions={0}, use_global_device_ids=true | all-gather | bytes 208896 | tf_op jit(solution)/shard_map/while/body/eval_jaxpr/all_gather | solution.py:93
  666.8 48.4 %all-gather.4 = bf16[16,192,32]{1,2,0:T(8,128)(2,1)S(1)} all-gather(bf16[1,192,32]{1,2,0:T(8,128)(2,1)S(1)} %fusion.37), channel_id=1, replica_groups=mesh['section'=16,'seq'=16,'cfg'=2] {'seq'}, dimensions={0}, use_global_device_ids=true | all-gather | bytes 208896 | tf_op jit(solution)/shard_map/while/body/eval_jaxpr/all_gather | solution.py:93
  774.1 48.4 %all-gather.4 = bf16[16,192,32]{1,2,0:T(8,128)(2,1)S(1)} all-gather(bf16[1,192,32]{1,2,0:T(8,128)(2,1)S(1)} %fusion.37), channel_id=1, replica_groups=mesh['section'=16,'seq'=16,'cfg'=2] {'seq'}, dimensions={0}, use_global_device_ids=true | all-gather | bytes 208896 | tf_op jit(solution)/shard_map/while/body/eval_jaxpr/all_gather | solution.py:93
  882.0 47.6 %all-gather.4 = bf16[16,192,32]{1,2,0:T(8,128)(2,1)S(1)} all-gather(bf16[1,192,32]{1,2,0:T(8,128)(2,1)S(1)} %fusion.37), channel_id=1, replica_groups=mesh['section'=16,'seq'=16,'cfg'=2] {'seq'}, dimensions={0}, use_global_device_ids=true | all-gather | bytes 208896 | tf_op jit(solution)/shard_map/while/body/eval_jaxpr/all_gather | solution.py:93
  933.7 47.3 %all-gather.5 = bf16[32,1,2048]{2,0,1:T(8,128)(2,1)S(1)} all-gather(bf16[32,1,128]{2,0,1:T(8,128)(2,1)S(1)} %fusion.41), channel_id=2, replica_groups=mesh['section'=16,'seq'=16,'cfg'=2] {'seq'}, dimensions={2}, use_global_device_ids=true | all-gather | bytes 139264 | tf_op jit(solution)/shard_map/while/body/eval_jaxpr/all_gather | solution.py:97
  989.7 47.5 %all-gather.4 = bf16[16,192,32]{1,2,0:T(8,128)(2,1)S(1)} all-gather(bf16[1,192,32]{1,2,0:T(8,128)(2,1)S(1)} %fusion.37), channel_id=1, replica_groups=mesh['section'=16,'seq'=16,'cfg'=2] {'seq'}, dimensions={0}, use_global_device_ids=true | all-gather | bytes 208896 | tf_op jit(solution)/shard_map/while/body/eval_jaxpr/all_gather | solution.py:93
  1041.3 47.1 %all-gather.5 = bf16[32,1,2048]{2,0,1:T(8,128)(2,1)S(1)} all-gather(bf16[32,1,128]{2,0,1:T(8,128)(2,1)S(1)} %fusion.41), channel_id=2, replica_groups=mesh['section'=16,'seq'=16,'cfg'=2] {'seq'}, dimensions={2}, use_global_device_ids=true | all-gather | bytes 139264 | tf_op jit(solution)/shard_map/while/body/eval_jaxpr/all_gather | solution.py:97
  1097.0 47.3 %all-gather.4 = bf16[16,192,32]{1,2,0:T(8,128)(2,1)S(1)} all-gather(bf16[1,192,32]{1,2,0:T(8,128)(2,1)S(1)} %fusion.37), channel_id=1, replica_groups=mesh['section'=16,'seq'=16,'cfg'=2] {'seq'}, dimensions={0}, use_global_device_ids=true | all-gather | bytes 208896 | tf_op jit(solution)/shard_map/while/body/eval_jaxpr/all_gather | solution.py:93
  1148.4 47.4 %all-gather.5 = bf16[32,1,2048]{2,0,1:T(8,128)(2,1)S(1)} all-gather(bf16[32,1,128]{2,0,1:T(8,128)(2,1)S(1)} %fusion.41), channel_id=2, replica_groups=mesh['section'=16,'seq'=16,'cfg'=2] {'seq'}, dimensions={2}, use_global_device_ids=true | all-gather | bytes 139264 | tf_op jit(solution)/shard_map/while/body/eval_jaxpr/all_gather | solution.py:97
  1204.5 47.2 %all-gather.4 = bf16[16,192,32]{1,2,0:T(8,128)(2,1)S(1)} all-gather(bf16[1,192,32]{1,2,0:T(8,128)(2,1)S(1)} %fusion.37), channel_id=1, replica_groups=mesh['section'=16,'seq'=16,'cfg'=2] {'seq'}, dimensions={0}, use_global_device_ids=true | all-gather | bytes 208896 | tf_op jit(solution)/shard_map/while/body/eval_jaxpr/all_gather | solution.py:93
  1255.8 47.2 %all-gather.5 = bf16[32,1,2048]{2,0,1:T(8,128)(2,1)S(1)} all-gather(bf16[32,1,128]{2,0,1:T(8,128)(2,1)S(1)} %fusion.41), channel_id=2, replica_groups=mesh['section'=16,'seq'=16,'cfg'=2] {'seq'}, dimensions={2}, use_global_device_ids=true | all-gather | bytes 139264 | tf_op jit(solution)/shard_map/while/body/eval_jaxpr/all_gather | solution.py:97
  1311.7 47.5 %all-gather.4 = bf16[16,192,32]{1,2,0:T(8,128)(2,1)S(1)} all-gather(bf16[1,192,32]{1,2,0:T(8,128)(2,1)S(1)} %fusion.37), channel_id=1, replica_groups=mesh['section'=16,'seq'=16,'cfg'=2] {'seq'}, dimensions={0}, use_global_device_ids=true | all-gather | bytes 208896 | tf_op jit(solution)/shard_map/while/body/eval_jaxpr/all_gather | solution.py:93
  1363.3 47.2 %all-gather.5 = bf16[32,1,2048]{2,0,1:T(8,128)(2,1)S(1)} all-gather(bf16[32,1,128]{2,0,1:T(8,128)(2,1)S(1)} %fusion.41), channel_id=2, replica_groups=mesh['section'=16,'seq'=16,'cfg'=2] {'seq'}, dimensions={2}, use_global_device_ids=true | all-gather | bytes 139264 | tf_op jit(solution)/shard_map/while/body/eval_jaxpr/all_gather | solution.py:97
  1419.1 47.5 %all-gather.4 = bf16[16,192,32]{1,2,0:T(8,128)(2,1)S(1)} all-gather(bf16[1,192,32]{1,2,0:T(8,128)(2,1)S(1)} %fusion.37), channel_id=1, replica_groups=mesh['section'=16,'seq'=16,'cfg'=2] {'seq'}, dimensions={0}, use_global_device_ids=true | all-gather | bytes 208896 | tf_op jit(solution)/shard_map/while/body/eval_jaxpr/all_gather | solution.py:93
  1470.7 47.0 %all-gather.5 = bf16[32,1,2048]{2,0,1:T(8,128)(2,1)S(1)} all-gather(bf16[32,1,128]{2,0,1:T(8,128)(2,1)S(1)} %fusion.41), channel_id=2, replica_groups=mesh['section'=16,'seq'=16,'cfg'=2] {'seq'}, dimensions={2}, use_global_device_ids=true | all-gather | bytes 139264 | tf_op jit(solution)/shard_map/while/body/eval_jaxpr/all_gather | solution.py:97
  1526.4 47.5 %all-gather.4 = bf16[16,192,32]{1,2,0:T(8,128)(2,1)S(1)} all-gather(bf16[1,192,32]{1,2,0:T(8,128)(2,1)S(1)} %fusion.37), channel_id=1, replica_groups=mesh['section'=16,'seq'=16,'cfg'=2] {'seq'}, dimensions={0}, use_global_device_ids=true | all-gather | bytes 208896 | tf_op jit(solution)/shard_map/while/body/eval_jaxpr/all_gather | solution.py:93
  1633.6 47.5 %all-gather.4 = bf16[16,192,32]{1,2,0:T(8,128)(2,1)S(1)} all-gather(bf16[1,192,32]{1,2,0:T(8,128)(2,1)S(1)} %fusion.37), channel_id=1, replica_groups=mesh['section'=16,'seq'=16,'cfg'=2] {'seq'}, dimensions={0}, use_global_device_ids=true | all-gather | bytes 208896 | tf_op jit(solution)/shard_map/while/body/eval_jaxpr/all_gather | solution.py:93
  1740.7 47.4 %all-gather.4 = bf16[16,192,32]{1,2,0:T(8,128)(2,1)S(1)} all-gather(bf16[1,192,32]{1,2,0:T(8,128)(2,1)S(1)} %fusion.37), channel_id=1, replica_groups=mesh['section'=16,'seq'=16,'cfg'=2] {'seq'}, dimensions={0}, use_global_device_ids=true | all-gather | bytes 208896 | tf_op jit(solution)/shard_map/while/body/eval_jaxpr/all_gather | solution.py:93
  (450 shorter events, 735.2 us)
Async XLA Ops:
  5.9 3.9 copy-start
  120.7 8.3 collective-permute-start
  228.3 8.5 collective-permute-start
  336.4 8.3 collective-permute-start
  443.7 8.3 collective-permute-start
  551.0 8.3 collective-permute-start
  658.3 8.5 collective-permute-start
  765.7 8.4 collective-permute-start
  873.7 8.3 collective-permute-start
  981.3 8.3 collective-permute-start
  1088.7 8.3 collective-permute-start
  1196.1 8.4 collective-permute-start
  1303.3 8.3 collective-permute-start
  1410.7 8.4 collective-permute-start
  1518.1 8.3 collective-permute-start
  1625.2 8.3 collective-permute-start
  1732.4 8.3 collective-permute-start
  1839.4 8.3 collective-permute-start
  1847.8 0.6 copy-start.1
where the time goes:
time: 1850 us
  blocking collectives  1620 us (88%)
  waiting for transfers between devices  107 us (6%)
  matrix products  49.1 us (3%)
  starting transfers between devices  34.2 us (2%)
    all_gather x17, blocking collectives, run_tick(): whole_rows = lax.all_gather(patch_rows, 'seq', axis=1, tiled=True)  827 us
    all_gather x17, blocking collectives, run_tick(): update = project(lax.all_gather(attended, 'seq', axis=1, tiled=True))  795 us
    ppermute x17, waiting for transfers between devices, passed_along(): return lax.ppermute(block, axis, route)  107 us
  transfers between devices with their start and end apart: 17, of which 17 were waited for; matrix products, arithmetic and copies ran while one was open for 0% of the time, Pallas kernels for 0%

commit v1 on v0

v1 whole, which is shorter than its diff:
```python
import jax
import jax.numpy as jnp
from jax import lax
from jax.experimental import pallas as pl
from jax.experimental.pallas import tpu as pltpu
from jax.sharding import PartitionSpec as P

D = 3072
HEAD_DIM = 128
INNER = 2048
PATCHES = 2
PATCH_TOK = 32
TOKENS = 64
WIDTH = 192
ZS = 4
YS = 4
SEQ = 16
LAYERS = 16
EPS_NORM = 1e-06
MESH = pl.DeviceIdType.MESH


def kernel(
    t_ref, latent, mod, wq, wo, stale,
    hid_out, kv_out,
    wbuf, wobuf, modbuf, vecs, cache, hb, att, own, nrm,
    ld_sem, h_send, h_recv, a_send, a_recv,
):
    sec = lax.axis_index("section")
    me = lax.axis_index("seq")
    cfg = lax.axis_index("cfg")
    zh = me // YS
    y = lax.rem(me, YS)

    loads = [
        pltpu.make_async_copy(mod, modbuf, ld_sem.at[0]),
        pltpu.make_async_copy(stale, cache, ld_sem.at[1]),
        pltpu.make_async_copy(latent, own, ld_sem.at[2]),
        pltpu.make_async_copy(wo, wobuf, ld_sem.at[3]),
    ]
    for part in range(3):
        for col in range(YS):
            loads.append(
                pltpu.make_async_copy(
                    wq.at[part, :, col],
                    wbuf.at[col, :, :, pl.ds(part * HEAD_DIM, HEAD_DIM)],
                    ld_sem.at[4 + part * YS + col],
                )
            )
    for one in loads:
        one.start()

    barrier = pltpu.get_barrier_semaphore()

    def greet_own(j, _):
        pl.semaphore_signal(
            barrier, inc=1, device_id=(sec, lax.rem(me + j, SEQ), cfg), device_id_type=MESH
        )
        return 0

    lax.fori_loop(1, SEQ, greet_own, 0)

    @pl.when(sec > 0)
    def _():
        def greet_before(j, _):
            pl.semaphore_signal(
                barrier, inc=1, device_id=(sec - 1, j, cfg), device_id_type=MESH
            )
            return 0

        lax.fori_loop(0, SEQ, greet_before, 0)

    loads[0].wait()
    pick = lax.broadcasted_iota(jnp.int32, (8, D), 0) == t_ref[0]
    for part in range(3):
        row = jnp.sum(
            jnp.where(pick, modbuf[part].astype(jnp.float32), 0.0), axis=0, keepdims=True
        )
        row = jnp.concatenate(
            [
                row[:, (z * YS + col) * WIDTH : (z * YS + col + 1) * WIDTH]
                for col in range(YS)
                for z in range(ZS)
            ],
            axis=1,
        )
        vecs[part] = row + 1.0 if part == 1 else row
    loads[1].wait()
    loads[2].wait()

    @pl.when(sec < LAYERS - 1)
    def _():
        pl.semaphore_wait(barrier, 2 * SEQ - 1)

    @pl.when(sec == LAYERS - 1)
    def _():
        pl.semaphore_wait(barrier, SEQ - 1)

    def rows(patch):
        return pl.ds(patch * PATCH_TOK, PATCH_TOK)

    def h_copy(patch, section, to):
        return pltpu.make_async_remote_copy(
            src_ref=own.at[rows(patch)],
            dst_ref=hb.at[patch, me],
            send_sem=h_send.at[patch, to],
            recv_sem=h_recv.at[patch, me],
            device_id=(section, to, cfg),
            device_id_type=MESH,
        )

    def a_copy(patch, to):
        mine = att.at[patch, zh, :, pl.ds(pl.multiple_of(y * HEAD_DIM, HEAD_DIM), HEAD_DIM)]
        return pltpu.make_async_remote_copy(
            src_ref=mine,
            dst_ref=mine,
            send_sem=a_send.at[patch, to],
            recv_sem=a_recv.at[patch, me],
            device_id=(sec, to, cfg),
            device_id_type=MESH,
        )

    def a_landing(patch, source):
        place = att.at[
            patch,
            source // YS,
            :,
            pl.ds(pl.multiple_of(lax.rem(source, YS) * HEAD_DIM, HEAD_DIM), HEAD_DIM),
        ]
        return pltpu.make_async_remote_copy(
            src_ref=place,
            dst_ref=place,
            send_sem=a_send.at[patch, source],
            recv_sem=a_recv.at[patch, source],
            device_id=(sec, source, cfg),
            device_id_type=MESH,
        )

    def h_landing(patch, source):
        return pltpu.make_async_remote_copy(
            src_ref=own.at[rows(patch)],
            dst_ref=hb.at[patch, source],
            send_sem=h_send.at[patch, source],
            recv_sem=h_recv.at[patch, source],
            device_id=(sec, source, cfg),
            device_id_type=MESH,
        )

    def each_peer(act, with_self):
        for dz in (2, 1, 3, 0):
            def one(j, _, dz=dz):
                act(lax.rem(zh + dz, ZS) * YS + lax.rem(y + j, YS))
                return 0

            lax.fori_loop(1 if dz == 0 and not with_self else 0, YS, one, 0)

    @pl.when(sec == 0)
    def _():
        for patch in range(PATCHES):
            each_peer(lambda to: h_copy(patch, sec, to).start(), False)
            hb[patch, me] = own[rows(patch)]
        for patch in range(PATCHES):
            each_peer(lambda to: h_landing(patch, to).wait_recv(), False)
        for patch in range(PATCHES):
            each_peer(lambda to: h_copy(patch, sec, to).wait_send(), False)

    def front(patch):
        @pl.when(sec > 0)
        def _():
            each_peer(lambda to: h_landing(patch, to).wait_recv(), True)

        whole = jnp.concatenate(
            [
                hb[patch, z * YS + col].astype(jnp.float32)
                for col in range(YS)
                for z in range(ZS)
            ],
            axis=1,
        )
        centred = whole - jnp.mean(whole, axis=-1, keepdims=True)
        spread = jnp.mean(centred * centred, axis=-1, keepdims=True)
        nrm[...] = (
            centred * (1.0 / jnp.sqrt(spread + EPS_NORM)) * vecs[1] + vecs[0]
        ).astype(jnp.bfloat16)
        if patch == 0:
            for one in loads[4:]:
                one.wait()
        projected = jnp.dot(
            nrm[...], wbuf[...].reshape(D, 3 * HEAD_DIM), preferred_element_type=jnp.float32
        )

        def rms(values):
            square = jnp.mean(values * values, axis=-1, keepdims=True)
            return (values * (1.0 / jnp.sqrt(square + EPS_NORM))).astype(jnp.bfloat16)

        query = rms(projected[:, :HEAD_DIM])
        cache[0, rows(patch), :] = rms(projected[:, HEAD_DIM : 2 * HEAD_DIM])
        cache[1, rows(patch), :] = projected[:, 2 * HEAD_DIM :].astype(jnp.bfloat16)
        scores = lax.dot_general(
            query, cache[0], (((1,), (1,)), ((), ())), preferred_element_type=jnp.float32
        )
        exponent = jnp.exp(scores * HEAD_DIM ** (-0.5))
        probs = (exponent * (1.0 / jnp.sum(exponent, axis=-1, keepdims=True))).astype(
            jnp.bfloat16
        )
        attended = jnp.dot(probs, cache[1], preferred_element_type=jnp.float32)
        att[
            patch, zh, :, pl.ds(pl.multiple_of(y * HEAD_DIM, HEAD_DIM), HEAD_DIM)
        ] = attended.astype(jnp.bfloat16)
        each_peer(lambda to: a_copy(patch, to).start(), False)

    def back(patch):
        if patch == 0:
            loads[3].wait()
        mine = vecs[2, :, pl.ds(pl.multiple_of(y * ZS * WIDTH, ZS * WIDTH), ZS * WIDTH)]
        gate = jnp.zeros((1, WIDTH), jnp.float32)
        for z in range(ZS):
            gate = gate + jnp.where(zh == z, mine[:, z * WIDTH : (z + 1) * WIDTH], 0.0)
        each_peer(lambda to: a_landing(patch, to).wait_recv(), False)
        update = jnp.zeros((PATCH_TOK, WIDTH), jnp.float32)
        for z in range(ZS):
            update = update + lax.dot_general(
                att[patch, z],
                wobuf[:, z * YS * HEAD_DIM : (z + 1) * YS * HEAD_DIM],
                (((1,), (1,)), ((), ())),
                preferred_element_type=jnp.float32,
            )
        result = (hb[patch, me].astype(jnp.float32) + gate * update).astype(jnp.bfloat16)
        own[rows(patch)] = result
        hid_out[rows(patch), :] = result

        @pl.when(sec < LAYERS - 1)
        def _():
            each_peer(lambda to: h_copy(patch, sec + 1, to).start(), True)

    for patch in range(PATCHES):
        front(patch)
    for patch in range(PATCHES):
        back(patch)
    kv_out[...] = cache[...]
    for patch in range(PATCHES):
        each_peer(lambda to: a_copy(patch, to).wait_send(), False)

        @pl.when(sec < LAYERS - 1)
        def _():
            each_peer(lambda to: h_copy(patch, sec + 1, to).wait_send(), True)


def on_device(latent, timestep, modulation, qkv_weight, out_weight, stale_kv):
    any_space = pl.BlockSpec(memory_space=pl.ANY)
    in_vmem = pl.BlockSpec(memory_space=pltpu.VMEM)
    bf16 = jnp.bfloat16
    hidden, caches = pl.pallas_call(
        kernel,
        out_shape=(
            jax.ShapeDtypeStruct((TOKENS, WIDTH), bf16),
            jax.ShapeDtypeStruct((2, TOKENS, HEAD_DIM), bf16),
        ),
        in_specs=[pl.BlockSpec(memory_space=pltpu.SMEM)] + [any_space] * 5,
        out_specs=(in_vmem, in_vmem),
        scratch_shapes=[
            pltpu.VMEM((YS, ZS, WIDTH, 3 * HEAD_DIM), bf16),
            pltpu.VMEM((WIDTH, INNER), bf16),
            pltpu.VMEM((3, 8, D), bf16),
            pltpu.VMEM((3, 1, D), jnp.float32),
            pltpu.VMEM((2, TOKENS, HEAD_DIM), bf16),
            pltpu.VMEM((PATCHES, SEQ, PATCH_TOK, WIDTH), bf16),
            pltpu.VMEM((PATCHES, ZS, PATCH_TOK, YS * HEAD_DIM), bf16),
            pltpu.VMEM((TOKENS, WIDTH), bf16),
            pltpu.VMEM((PATCH_TOK, D), bf16),
            pltpu.SemaphoreType.DMA((16,)),
            pltpu.SemaphoreType.DMA((PATCHES, SEQ)),
            pltpu.SemaphoreType.DMA((PATCHES, SEQ)),
            pltpu.SemaphoreType.DMA((PATCHES, SEQ)),
            pltpu.SemaphoreType.DMA((PATCHES, SEQ)),
        ],
        compiler_params=pltpu.CompilerParams(
            collective_id=0, has_side_effects=True, vmem_limit_bytes=48 * 1024 * 1024
        ),
    )(
        timestep,
        latent,
        modulation[0].transpose(1, 0, 2),
        qkv_weight[0].transpose(1, 0, 2).reshape(3, ZS, YS, WIDTH, HEAD_DIM),
        out_weight[0].transpose(1, 0),
        stale_kv[0],
    )
    return hidden[None], caches[None]


def solution(mesh):
    placed = (
        P(None, "seq"),
        P(),
        P("section", "cfg", None, None),
        P("section", None, None, "seq"),
        P("section", None, "seq"),
        P("section", None, "cfg", "seq"),
    )
    return jax.shard_map(
        on_device,
        mesh=mesh,
        in_specs=placed,
        out_specs=(P("section", "cfg", "seq"), P("section", None, "cfg", "seq")),
        check_vma=False,
    )
```

time: 1850 us -> 349 us (0.19)
  the two profiles are of different devices: /device:TPU:6 before, /device:TPU:102 now
where the time goes in v1:
time: 349 us
  Pallas kernels  341 us (98%)
  local copies, waits for them, and re-layouts  6.45 us (2%)
    pallas_call x1, Pallas kernels, on_device(): pl.pallas_call(kernel, out_shape=(jax.ShapeDtypeStruct((TOKENS, WIDTH), b...  341 us

profile of v1, /device:TPU:102, one launch (start us, length us, event | category | flops | bytes accessed | tf_op | source)
XLA Modules:
  0.0 348.9 jit_solution(3383434573912696129)
XLA Ops:
  1.3 0.0 copy-start
  1.3 1.7 copy-done
  2.9 0.0 copy-start.1
  2.9 1.1 copy-done.1
  4.1 0.0 copy-start.2
  4.1 0.9 copy-done.2
  5.0 0.0 copy-start.3
  5.0 0.8 copy-done.3
  5.7 0.0 copy-start.4
  5.7 0.8 copy-done.4
  6.5 341.1 %shard_map.77 = (bf16[64,192]{1,0:T(8,128)(2,1)S(1)}, bf16[2,64,128]{2,1,0:T(8,128)(2,1)S(1)}) custom-call(s32[1]{0:T(128)S(6)} %copy.10.t_ref, bf16[64,192]{1,0:T(8,128)(2,1)S(1)} %copy-done.3, bf16[3,8,3072]{2,1,0:T(8,128)(2,1)S(1)} %bitcast.16, bf16[3,4,4,192,128]{4,3,2,1,0:T(8,128)(2,1)S(1)} %bitcast.14, bf16[192,2048]{1,0:T(8,128)(2,1)S(1)} %bitcast.15, ...), custom_call_target="tpu_custom_call" | custom-call | tf_op jit(solution)/shard_map/pallas_call | solution.py:253
  347.6 0.6 copy.11
  348.2 0.6 copy.12
Async XLA Ops:
  1.3 1.7 copy-start
  2.9 1.1 copy-start.1
  4.1 0.9 copy-start.2
  5.0 0.8 copy-start.3
  5.7 0.8 copy-start.4

commit v2 on v1

v2 whole, which is shorter than its diff:
```python
import jax
import jax.numpy as jnp
from jax import lax
from jax.experimental import pallas as pl
from jax.experimental.pallas import tpu as pltpu
from jax.sharding import PartitionSpec as P

D = 3072
HEAD_DIM = 128
INNER = 2048
PATCHES = 2
PATCH_TOK = 32
TOKENS = 64
WIDTH = 192
ZS = 4
YS = 4
SEQ = 16
LAYERS = 16
GROUP = ZS * HEAD_DIM
WIDE = ZS * WIDTH
EPS_NORM = 1e-06
MESH = pl.DeviceIdType.MESH

FIRST = 2
HOST = (0, 0, 0, 1, 2, 3, 0, 1, 2, 2, 3, 3, 0, 0, 1, 1)
CHUNKS = 3 * YS + 1


def host_of(section):
    place = section * 0
    for layer in range(LAYERS):
        if HOST[layer]:
            place = jnp.where(section == layer, HOST[layer], place)
    return place


def kernel(
    t_ref, latent, mod, wq, wo, stale,
    hid_out, kv_out,
    wbuf, wobuf, modbuf, vecs, cache, hb, hwide, att, own, wide, hst, hland, kvland, nrm,
    ld_sem, h_send, h_recv, a_send, a_recv,
    w_send, w_recv, f_send, f_recv, s_send, s_recv, o_send, o_recv,
):
    sec = lax.axis_index("section")
    me = lax.axis_index("seq")
    cfg = lax.axis_index("cfg")
    zh = me // YS
    y = lax.rem(me, YS)
    place = host_of(sec)
    spread = sec < FIRST
    hosting = (sec >= FIRST) & (zh == place)
    helping = (sec >= FIRST) & (zh != place)

    def rows(patch):
        return pl.ds(patch * PATCH_TOK, PATCH_TOK)

    def lanes(number, size=HEAD_DIM):
        return pl.ds(pl.multiple_of(number * size, size), size)

    def remote(src, dst, send, recv, device):
        return pltpu.make_async_remote_copy(
            src_ref=src, dst_ref=dst, send_sem=send, recv_sem=recv,
            device_id=device, device_id_type=MESH,
        )

    def greet(device):
        pl.semaphore_signal(barrier, inc=1, device_id=device, device_id_type=MESH)

    def loop(low, high, act):
        def one(j, _):
            act(j)
            return 0

        lax.fori_loop(low, high, one, 0)

    def each_peer(act, with_self):
        for dz in (2, 1, 3, 0):
            loop(
                1 if dz == 0 and not with_self else 0,
                YS,
                lambda j, dz=dz: act(lax.rem(zh + dz, ZS) * YS + lax.rem(y + j, YS)),
            )

    def each_ring(act, with_self):
        for dy in (2, 1, 3, 0) if with_self else (2, 1, 3):
            act(lax.rem(y + dy, YS))

    def each_helper(act):
        loop(1, ZS, lambda j: act(lax.rem(place + j, ZS)))

    loads = [
        pltpu.make_async_copy(mod, modbuf, ld_sem.at[0]),
        pltpu.make_async_copy(stale, cache.at[zh], ld_sem.at[1]),
        pltpu.make_async_copy(latent, own, ld_sem.at[2]),
        pltpu.make_async_copy(
            wo, wobuf.at[pl.ds(pl.multiple_of(zh * WIDTH, WIDTH), WIDTH)], ld_sem.at[3]
        ),
    ]
    for part in range(3):
        for col in range(YS):
            loads.append(
                pltpu.make_async_copy(
                    wq.at[part, :, col],
                    wbuf.at[col, :, :, lanes(part * ZS + zh)],
                    ld_sem.at[4 + part * YS + col],
                )
            )

    @pl.when(jnp.logical_not(helping))
    def _():
        for one in loads:
            one.start()

    barrier = pltpu.get_barrier_semaphore()

    @pl.when(spread)
    def _():
        each_peer(lambda to: greet((sec, to, cfg)), False)

        @pl.when(sec > 0)
        def _():
            loop(0, SEQ, lambda j: greet((sec - 1, j, cfg)))

    @pl.when(hosting)
    def _():
        each_helper(lambda z: greet((sec, z * YS + y, cfg)))
        greet((sec, me, 1 - cfg))
        each_ring(lambda col: greet((sec, place * YS + col, cfg)), False)

        @pl.when(sec == FIRST)
        def _():
            loop(0, SEQ, lambda j: greet((sec - 1, j, cfg)))

        @pl.when(sec > FIRST)
        def _():
            before = host_of(sec - 1) * YS
            loop(0, YS, lambda j: greet((sec - 1, before + j, cfg)))

    @pl.when(helping)
    def _():
        greet((sec, place * YS + y, cfg))
        pl.semaphore_wait(barrier, 1)

    @pl.when(sec < FIRST - 1)
    def _():
        pl.semaphore_wait(barrier, SEQ - 1 + SEQ)

    @pl.when(sec == FIRST - 1)
    def _():
        pl.semaphore_wait(barrier, SEQ - 1 + YS)

    @pl.when(hosting & (sec < LAYERS - 1))
    def _():
        pl.semaphore_wait(barrier, 2 * YS - 1 + ZS)

    @pl.when(hosting & (sec == LAYERS - 1))
    def _():
        pl.semaphore_wait(barrier, YS - 1 + ZS)

    def chunk_at(number, half, z):
        if number == CHUNKS - 1:
            return wobuf.at[
                pl.ds(pl.multiple_of(z * WIDTH, WIDTH), WIDTH), lanes(half, INNER // 2)
            ]
        part, col = divmod(number, YS)
        return wbuf.at[col, pl.ds(half * 2, 2), :, lanes(part * ZS + z)]

    def chunk_from(number, half):
        if number == CHUNKS - 1:
            return wo.at[:, lanes(half, INNER // 2)]
        part, col = divmod(number, YS)
        return wq.at[part, pl.ds(half * 2, 2), col]

    def w_copy(number):
        return remote(
            chunk_from(number, cfg), chunk_at(number, cfg, zh),
            w_send.at[number], w_recv.at[zh, number], (sec, place * YS + y, cfg),
        )

    def w_landing(number, z):
        spot = chunk_at(number, cfg, z)
        return remote(
            spot, spot, w_send.at[number], w_recv.at[z, number], (sec, z * YS + y, cfg)
        )

    def swap(number, z, half):
        spot = chunk_at(number, half, z)
        return remote(
            spot, spot, f_send.at[z, number], f_recv.at[z, number], (sec, me, 1 - cfg)
        )

    def s_copy():
        return remote(
            stale, cache.at[zh], s_send, s_recv.at[zh], (sec, place * YS + y, cfg)
        )

    def s_landing(z):
        return remote(
            stale, cache.at[z], s_send, s_recv.at[z], (sec, z * YS + y, cfg)
        )

    def o_copy(z, number):
        src = cache.at[z] if number == 2 else hst.at[z, rows(number)]
        dst = kvland if number == 2 else hland.at[rows(number)]
        return remote(src, dst, o_send.at[z, number], o_recv.at[number], (sec, z * YS + y, cfg))

    @pl.when(helping)
    def _():
        s_copy().start()
        for number in range(CHUNKS):
            w_copy(number).start()
        for number in range(CHUNKS):
            w_copy(number).wait_send()
        s_copy().wait_send()
        for number in range(3):
            o_copy(zh, number).wait_recv()
        hid_out[...] = hland[...]
        kv_out[...] = kvland[...]

    def h_copy(patch, section, to):
        return remote(
            own.at[rows(patch)], hb.at[patch, me],
            h_send.at[patch, to], h_recv.at[patch, me], (section, to, cfg),
        )

    def h_landing(patch, source):
        return remote(
            own.at[rows(patch)], hb.at[patch, source],
            h_send.at[patch, source], h_recv.at[patch, source], (sec, source, cfg),
        )

    def wide_copy(patch, to, col):
        return remote(
            wide.at[patch], hwide.at[patch, y],
            h_send.at[patch, col], h_recv.at[patch, y], (sec + 1, to * YS + col, cfg),
        )

    def wide_landing(patch, col):
        return remote(
            wide.at[patch], hwide.at[patch, col],
            h_send.at[patch, col], h_recv.at[patch, col], (sec, col, cfg),
        )

    def a_copy(patch, source, to):
        spot = att.at[patch, source // YS, :, lanes(lax.rem(source, YS))]
        return remote(
            spot, spot, a_send.at[patch, to], a_recv.at[patch, source], (sec, to, cfg)
        )

    def ring_copy(patch, source, to):
        spot = att.at[patch, :, :, lanes(source)]
        return remote(
            spot, spot, a_send.at[patch, to], a_recv.at[patch, source],
            (sec, place * YS + to, cfg),
        )

    def rms(values):
        square = jnp.mean(values * values, axis=-1, keepdims=True)
        return (values * (1.0 / jnp.sqrt(square + EPS_NORM))).astype(jnp.bfloat16)

    def modulation_rows():
        loads[0].wait()
        pick = lax.broadcasted_iota(jnp.int32, (8, D), 0) == t_ref[0]
        for part in range(3):
            row = jnp.sum(
                jnp.where(pick, modbuf[part].astype(jnp.float32), 0.0), axis=0, keepdims=True
            )
            row = jnp.concatenate(
                [
                    row[:, (z * YS + col) * WIDTH : (z * YS + col + 1) * WIDTH]
                    for col in range(YS)
                    for z in range(ZS)
                ],
                axis=1,
            )
            vecs[part] = row + 1.0 if part == 1 else row

    def assemble(patch):
        for col in range(YS):
            hwide[patch, col] = jnp.concatenate(
                [hb[patch, z * YS + col].astype(jnp.float32) for z in range(ZS)], axis=1
            ).astype(jnp.bfloat16)

    def normalise(patch):
        whole = jnp.concatenate(
            [hwide[patch, col].astype(jnp.float32) for col in range(YS)], axis=1
        )
        centred = whole - jnp.mean(whole, axis=-1, keepdims=True)
        spread_of = jnp.mean(centred * centred, axis=-1, keepdims=True)
        nrm[...] = (
            centred * (1.0 / jnp.sqrt(spread_of + EPS_NORM)) * vecs[1] + vecs[0]
        ).astype(jnp.bfloat16)

    def attend(patch, z, query, key, value):
        cache[z, 0, rows(patch), :] = rms(key)
        cache[z, 1, rows(patch), :] = value.astype(jnp.bfloat16)
        scores = lax.dot_general(
            rms(query), cache[z, 0], (((1,), (1,)), ((), ())),
            preferred_element_type=jnp.float32,
        )
        exponent = jnp.exp(scores * HEAD_DIM ** (-0.5))
        probs = (exponent * (1.0 / jnp.sum(exponent, axis=-1, keepdims=True))).astype(
            jnp.bfloat16
        )
        attended = jnp.dot(probs, cache[z, 1], preferred_element_type=jnp.float32)
        att[patch, z, :, lanes(y)] = attended.astype(jnp.bfloat16)

    def project_out(patch, weight):
        update = None
        for z in range(ZS):
            term = lax.dot_general(
                att[patch, z], weight(z), (((1,), (1,)), ((), ())),
                preferred_element_type=jnp.float32,
            )
            update = term if update is None else update + term
        return update

    @pl.when(spread)
    def _():
        modulation_rows()
        loads[1].wait()
        loads[2].wait()

        @pl.when(sec == 0)
        def _():
            for patch in range(PATCHES):
                each_peer(lambda to: h_copy(patch, sec, to).start(), False)
                hb[patch, me] = own[rows(patch)]
            for patch in range(PATCHES):
                each_peer(lambda to: h_landing(patch, to).wait_recv(), False)
            for patch in range(PATCHES):
                each_peer(lambda to: h_copy(patch, sec, to).wait_send(), False)

        def front(patch):
            @pl.when(sec > 0)
            def _():
                each_peer(lambda to: h_landing(patch, to).wait_recv(), True)

            assemble(patch)
            normalise(patch)
            if patch == 0:
                for one in loads[4:]:
                    one.wait()
            projected = [
                jnp.dot(
                    nrm[...],
                    wbuf[:, :, :, lanes(part * ZS + zh)].reshape(D, HEAD_DIM),
                    preferred_element_type=jnp.float32,
                )
                for part in range(3)
            ]
            attend(patch, zh, *projected)
            each_peer(lambda to: a_copy(patch, me, to).start(), False)

        def back(patch):
            if patch == 0:
                loads[3].wait()
            mine = vecs[2, :, lanes(y, WIDE)]
            gate = jnp.zeros((1, WIDTH), jnp.float32)
            for z in range(ZS):
                gate = gate + jnp.where(zh == z, mine[:, z * WIDTH : (z + 1) * WIDTH], 0.0)
            each_peer(lambda to: a_copy(patch, to, to).wait_recv(), False)
            part = pl.ds(pl.multiple_of(zh * WIDTH, WIDTH), WIDTH)
            update = project_out(patch, lambda z: wobuf[part, z * GROUP : (z + 1) * GROUP])
            result = (hb[patch, me].astype(jnp.float32) + gate * update).astype(jnp.bfloat16)
            own[rows(patch)] = result

            @pl.when(sec < FIRST - 1)
            def _():
                each_peer(lambda to: h_copy(patch, sec + 1, to).start(), True)

            @pl.when(sec == FIRST - 1)
            def _():
                each_ring(
                    lambda col: h_copy(patch, sec + 1, HOST[FIRST] * YS + col).start(), True
                )

            hid_out[rows(patch), :] = result

        for patch in range(PATCHES):
            front(patch)
        for patch in range(PATCHES):
            back(patch)
        kv_out[...] = cache[zh]
        for patch in range(PATCHES):
            each_peer(lambda to: a_copy(patch, me, to).wait_send(), False)

            @pl.when(sec < FIRST - 1)
            def _():
                each_peer(lambda to: h_copy(patch, sec + 1, to).wait_send(), True)

            @pl.when(sec == FIRST - 1)
            def _():
                each_ring(
                    lambda col: h_copy(patch, sec + 1, HOST[FIRST] * YS + col).wait_send(), True
                )

    @pl.when(hosting)
    def _():
        modulation_rows()
        for one in loads[1:]:
            one.wait()
        for number in range(CHUNKS):
            def relay(z, number=number):
                w_landing(number, z).wait_recv()
                swap(number, z, cfg).start()

            each_helper(relay)
        each_helper(lambda z: s_landing(z).wait_recv())
        for number in range(CHUNKS):
            each_helper(lambda z: swap(number, z, 1 - cfg).wait_recv())
            each_helper(lambda z: swap(number, z, cfg).wait_send())
        after = host_of(sec + 1)

        def front(patch):
            @pl.when(sec == FIRST)
            def _():
                loop(0, SEQ, lambda j: h_landing(patch, j).wait_recv())
                assemble(patch)

            @pl.when(sec > FIRST)
            def _():
                loop(0, YS, lambda j: wide_landing(patch, j).wait_recv())

            normalise(patch)
            projected = jnp.dot(
                nrm[...], wbuf[...].reshape(D, 3 * GROUP), preferred_element_type=jnp.float32
            )
            for z in range(ZS):
                attend(
                    patch, z,
                    *[
                        projected[:, part * GROUP + z * HEAD_DIM : part * GROUP + (z + 1) * HEAD_DIM]
                        for part in range(3)
                    ],
                )
            each_ring(lambda col: ring_copy(patch, y, col).start(), False)

        def back(patch):
            each_ring(lambda col: ring_copy(patch, col, col).wait_recv(), False)
            update = project_out(patch, lambda z: wobuf[:, z * GROUP : (z + 1) * GROUP])
            result = hwide[patch, y].astype(jnp.float32) + vecs[2, :, lanes(y, WIDE)] * update
            wide[patch] = result.astype(jnp.bfloat16)

            @pl.when(sec < LAYERS - 1)
            def _():
                each_ring(lambda col: wide_copy(patch, after, col).start(), True)

            for z in range(ZS):
                hst[z, rows(patch)] = result[:, z * WIDTH : (z + 1) * WIDTH].astype(jnp.bfloat16)
            each_helper(lambda z: o_copy(z, patch).start())

        for patch in range(PATCHES):
            front(patch)
        each_helper(lambda z: o_copy(z, 2).start())
        for patch in range(PATCHES):
            back(patch)
        kv_out[...] = cache[place]
        hid_out[...] = hst[place]
        for patch in range(PATCHES):
            each_ring(lambda col: ring_copy(patch, y, col).wait_send(), False)

            @pl.when(sec < LAYERS - 1)
            def _():
                each_ring(lambda col: wide_copy(patch, after, col).wait_send(), True)

        for number in range(3):
            each_helper(lambda z: o_copy(z, number).wait_send())


def on_device(latent, timestep, modulation, qkv_weight, out_weight, stale_kv):
    any_space = pl.BlockSpec(memory_space=pl.ANY)
    in_vmem = pl.BlockSpec(memory_space=pltpu.VMEM)
    bf16 = jnp.bfloat16
    dma = pltpu.SemaphoreType.DMA
    hidden, caches = pl.pallas_call(
        kernel,
        out_shape=(
            jax.ShapeDtypeStruct((TOKENS, WIDTH), bf16),
            jax.ShapeDtypeStruct((2, TOKENS, HEAD_DIM), bf16),
        ),
        in_specs=[pl.BlockSpec(memory_space=pltpu.SMEM)] + [any_space] * 5,
        out_specs=(in_vmem, in_vmem),
        scratch_shapes=[
            pltpu.VMEM((YS, ZS, WIDTH, 3 * GROUP), bf16),
            pltpu.VMEM((WIDE, INNER), bf16),
            pltpu.VMEM((3, 8, D), bf16),
            pltpu.VMEM((3, 1, D), jnp.float32),
            pltpu.VMEM((ZS, 2, TOKENS, HEAD_DIM), bf16),
            pltpu.VMEM((PATCHES, SEQ, PATCH_TOK, WIDTH), bf16),
            pltpu.VMEM((PATCHES, YS, PATCH_TOK, WIDE), bf16),
            pltpu.VMEM((PATCHES, ZS, PATCH_TOK, YS * HEAD_DIM), bf16),
            pltpu.VMEM((TOKENS, WIDTH), bf16),
            pltpu.VMEM((PATCHES, PATCH_TOK, WIDE), bf16),
            pltpu.VMEM((ZS, TOKENS, WIDTH), bf16),
            pltpu.VMEM((TOKENS, WIDTH), bf16),
            pltpu.VMEM((2, TOKENS, HEAD_DIM), bf16),
            pltpu.VMEM((PATCH_TOK, D), bf16),
            dma((16,)),
            dma((PATCHES, SEQ)),
            dma((PATCHES, SEQ)),
            dma((PATCHES, SEQ)),
            dma((PATCHES, SEQ)),
            dma((CHUNKS,)),
            dma((ZS, CHUNKS)),
            dma((ZS, CHUNKS)),
            dma((ZS, CHUNKS)),
            dma,
            dma((ZS,)),
            dma((ZS, 3)),
            dma((3,)),
        ],
        compiler_params=pltpu.CompilerParams(
            collective_id=0, has_side_effects=True, vmem_limit_bytes=60 * 1024 * 1024
        ),
    )(
        timestep,
        latent,
        modulation[0].transpose(1, 0, 2),
        qkv_weight[0].transpose(1, 0, 2).reshape(3, ZS, YS, WIDTH, HEAD_DIM),
        out_weight[0].transpose(1, 0),
        stale_kv[0],
    )
    return hidden[None], caches[None]


def solution(mesh):
    placed = (
        P(None, "seq"),
        P(),
        P("section", "cfg", None, None),
        P("section", None, None, "seq"),
        P("section", None, "seq"),
        P("section", None, "cfg", "seq"),
    )
    return jax.shard_map(
        on_device,
        mesh=mesh,
        in_specs=placed,
        out_specs=(P("section", "cfg", "seq"), P("section", None, "cfg", "seq")),
        check_vma=False,
    )
```

time: 349 us -> 336 us (0.963)
  Pallas kernels: 341 us -> 332 us
  local copies, waits for them, and re-layouts: 6.45 us -> 2.75 us
    pallas_call x1, Pallas kernels: 341 us -> 332 us  [on_device(): pl.pallas_call(kernel, out_shape=(jax.ShapeDtypeStruct((TOKENS, WIDTH), b...]
    unnamed x12 -> x2, local copies, waits for them, and re-layouts: 6.45 us -> 2.75 us
where the time goes in v2:
time: 336 us
  Pallas kernels  332 us (99%)
    pallas_call x1, Pallas kernels, on_device(): pl.pallas_call(kernel, out_shape=(jax.ShapeDtypeStruct((TOKENS, WIDTH), b...  332 us

profile of v2, /device:TPU:102, one launch (start us, length us, event | category | flops | bytes accessed | tf_op | source)
XLA Modules:
  0.0 335.9 jit_solution(11913387374991361755)
XLA Ops:
  1.3 331.9 %shard_map.77 = (bf16[64,192]{1,0:T(8,128)(2,1)}, bf16[2,64,128]{2,1,0:T(8,128)(2,1)}) custom-call(s32[1]{0:T(128)S(6)} %copy.10.t_ref, bf16[64,192]{1,0:T(8,128)(2,1)} %latent.1, bf16[3,8,3072]{2,1,0:T(8,128)(2,1)} %bitcast.16, bf16[3,4,4,192,128]{4,3,2,1,0:T(8,128)(2,1)} %bitcast.14, bf16[192,2048]{1,0:T(8,128)(2,1)} %bitcast.15, bf16[2,64,128]{2,1,0:T(8,128)(2,1)} %bitcast.17), custom_call_target="tpu_custom_call" | custom-call | tf_op jit(solution)/shard_map/pallas_call | solution.py:476
  333.1 1.4 copy.11
  334.5 1.4 copy.12

commit v3 on v2

--- a/solution.py
+++ b/solution.py
@@ -21,8 +21,8 @@
 EPS_NORM = 1e-06
 MESH = pl.DeviceIdType.MESH
 
-FIRST = 2
-HOST = (0, 0, 0, 1, 2, 3, 0, 1, 2, 2, 3, 3, 0, 0, 1, 1)
+FIRST = 5
+HOST = (0, 0, 0, 0, 0, 3, 0, 1, 2, 2, 3, 3, 0, 0, 1, 1)
 CHUNKS = 3 * YS + 1
 
 
@@ -38,6 +38,7 @@
     t_ref, latent, mod, wq, wo, stale,
     hid_out, kv_out,
     wbuf, wobuf, modbuf, vecs, cache, hb, hwide, att, own, wide, hst, hland, kvland, nrm,
+    wot, base, shifted,
     ld_sem, h_send, h_recv, a_send, a_recv,
     w_send, w_recv, f_send, f_recv, s_send, s_recv, o_send, o_recv,
 ):
@@ -291,19 +292,26 @@
             centred * (1.0 / jnp.sqrt(spread_of + EPS_NORM)) * vecs[1] + vecs[0]
         ).astype(jnp.bfloat16)
 
-    def attend(patch, z, query, key, value):
-        cache[z, 0, rows(patch), :] = rms(key)
-        cache[z, 1, rows(patch), :] = value.astype(jnp.bfloat16)
-        scores = lax.dot_general(
-            rms(query), cache[z, 0], (((1,), (1,)), ((), ())),
-            preferred_element_type=jnp.float32,
-        )
-        exponent = jnp.exp(scores * HEAD_DIM ** (-0.5))
-        probs = (exponent * (1.0 / jnp.sum(exponent, axis=-1, keepdims=True))).astype(
-            jnp.bfloat16
-        )
-        attended = jnp.dot(probs, cache[z, 1], preferred_element_type=jnp.float32)
-        att[patch, z, :, lanes(y)] = attended.astype(jnp.bfloat16)
+    def attend(patch, heads):
+        for z, _, key, value in heads:
+            cache[z, 0, rows(patch), :] = rms(key)
+            cache[z, 1, rows(patch), :] = value.astype(jnp.bfloat16)
+        queries = [rms(head[1]) for head in heads]
+        scores = [
+            lax.dot_general(
+                query, cache[head[0], 0], (((1,), (1,)), ((), ())),
+                preferred_element_type=jnp.float32,
+            )
+            for head, query in zip(heads, queries)
+        ]
+        exponents = [jnp.exp(score * HEAD_DIM ** (-0.5)) for score in scores]
+        sums = [1.0 / jnp.sum(exponent, axis=-1, keepdims=True) for exponent in exponents]
+        probs = [(top * below).astype(jnp.bfloat16) for top, below in zip(exponents, sums)]
+        attended = [
+            jnp.dot(prob, cache[head[0], 1], preferred_element_type=jnp.float32)
+            for head, prob in zip(heads, probs)
+        ]
+        return [block.astype(jnp.bfloat16) for block in attended]
 
     def project_out(patch, weight):
         update = None
@@ -326,12 +334,13 @@
             for patch in range(PATCHES):
                 each_peer(lambda to: h_copy(patch, sec, to).start(), False)
                 hb[patch, me] = own[rows(patch)]
-            for patch in range(PATCHES):
+
+        def front(patch):
+            @pl.when(sec == 0)
+            def _():
                 each_peer(lambda to: h_landing(patch, to).wait_recv(), False)
-            for patch in range(PATCHES):
                 each_peer(lambda to: h_copy(patch, sec, to).wait_send(), False)
 
-        def front(patch):
             @pl.when(sec > 0)
             def _():
                 each_peer(lambda to: h_landing(patch, to).wait_recv(), True)
@@ -349,7 +358,7 @@
                 )
                 for part in range(3)
             ]
-            attend(patch, zh, *projected)
+            att[patch, zh, :, lanes(y)] = attend(patch, [(zh, *projected)])[0]
             each_peer(lambda to: a_copy(patch, me, to).start(), False)
 
         def back(patch):
@@ -412,33 +421,82 @@
             each_helper(lambda z: swap(number, z, cfg).wait_send())
         after = host_of(sec + 1)
 
+        def turn(j):
+            at = lanes(j)
+            wot[at, :] = wobuf[:, at].T
+
+        loop(0, INNER // HEAD_DIM, turn)
+
+        which = lax.broadcasted_iota(jnp.int32, (16, WIDE), 0)
+        shift_sum = None
+        for col in range(YS):
+            here = slice(col * WIDE, (col + 1) * WIDE)
+            scale = vecs[1, :, here]
+            high = scale.astype(jnp.bfloat16).astype(jnp.float32)
+            stack = jnp.where(
+                which == 0, high,
+                jnp.where(which == 1, scale - high, jnp.where(which == 2, vecs[0, :, here], 0.0)),
+            )
+            sums = jnp.dot(
+                stack.astype(jnp.bfloat16), wbuf[col].reshape(WIDE, 3 * GROUP),
+                preferred_element_type=jnp.float32,
+            )
+            base[col] = sums[0:1] + sums[1:2]
+            shift_sum = sums[2:3] if shift_sum is None else shift_sum + sums[2:3]
+        shifted[...] = shift_sum
+
         def front(patch):
             @pl.when(sec == FIRST)
             def _():
                 loop(0, SEQ, lambda j: h_landing(patch, j).wait_recv())
                 assemble(patch)
 
-            @pl.when(sec > FIRST)
-            def _():
-                loop(0, YS, lambda j: wide_landing(patch, j).wait_recv())
-
-            normalise(patch)
-            projected = jnp.dot(
-                nrm[...], wbuf[...].reshape(D, 3 * GROUP), preferred_element_type=jnp.float32
-            )
-            for z in range(ZS):
-                attend(
-                    patch, z,
-                    *[
+            total, parts = None, []
+            for dy in (0, 1, 3, 2):
+                col = lax.rem(y + dy, YS)
+
+                @pl.when(sec > FIRST)
+                def _(col=col):
+                    wide_landing(patch, col).wait_recv()
+
+                block = hwide[patch, col].astype(jnp.float32)
+                middle = jnp.mean(block, axis=-1, keepdims=True)
+                block = block - middle
+                parts.append((col, middle, jnp.sum(block * block, axis=-1, keepdims=True)))
+                term = jnp.dot(
+                    (block * vecs[1, :, lanes(col, WIDE)]).astype(jnp.bfloat16),
+                    wbuf[col].reshape(WIDE, 3 * GROUP),
+                    preferred_element_type=jnp.float32,
+                )
+                total = term if total is None else total + term
+            mean = sum(part[1] for part in parts) * (1.0 / YS)
+            spread_of = sum(part[2] + WIDE * (part[1] - mean) ** 2 for part in parts) * (1.0 / D)
+            for col, middle, _ in parts:
+                total = total + (middle - mean) * base[col]
+            projected = total * (1.0 / jnp.sqrt(spread_of + EPS_NORM)) + shifted[...]
+            attended = attend(
+                patch,
+                [
+                    (z, *[
                         projected[:, part * GROUP + z * HEAD_DIM : part * GROUP + (z + 1) * HEAD_DIM]
                         for part in range(3)
-                    ],
-                )
+                    ])
+                    for z in range(ZS)
+                ],
+            )
+            for z in range(ZS):
+                att[patch, z, :, lanes(y)] = attended[z]
             each_ring(lambda col: ring_copy(patch, y, col).start(), False)
 
         def back(patch):
             each_ring(lambda col: ring_copy(patch, col, col).wait_recv(), False)
-            update = project_out(patch, lambda z: wobuf[:, z * GROUP : (z + 1) * GROUP])
+            update = None
+            for z in range(ZS):
+                term = jnp.dot(
+                    att[patch, z], wot[z * GROUP : (z + 1) * GROUP],
+                    preferred_element_type=jnp.float32,
+                )
+                update = term if update is None else update + term
             result = hwide[patch, y].astype(jnp.float32) + vecs[2, :, lanes(y, WIDE)] * update
             wide[patch] = result.astype(jnp.bfloat16)
 
@@ -496,6 +554,9 @@
             pltpu.VMEM((TOKENS, WIDTH), bf16),
             pltpu.VMEM((2, TOKENS, HEAD_DIM), bf16),
             pltpu.VMEM((PATCH_TOK, D), bf16),
+            pltpu.VMEM((INNER, WIDE), bf16),
+            pltpu.VMEM((YS, 1, 3 * GROUP), jnp.float32),
+            pltpu.VMEM((1, 3 * GROUP), jnp.float32),
             dma((16,)),
             dma((PATCHES, SEQ)),
             dma((PATCHES, SEQ)),

time: 336 us -> 278 us (0.83)
  Pallas kernels: 332 us -> 273 us
    pallas_call x1, Pallas kernels: 332 us -> 273 us  [on_device(): pl.pallas_call(kernel, out_shape=(jax.ShapeDtypeStruct((TOKENS, WIDTH), b...]
where the time goes in v3:
time: 278 us; the launch traced here: 277 us
  Pallas kernels  273 us (98%)
    pallas_call x1, Pallas kernels, on_device(): pl.pallas_call(kernel, out_shape=(jax.ShapeDtypeStruct((TOKENS, WIDTH), b...  273 us

profile of v3, /device:TPU:102, one launch (start us, length us, event | category | flops | bytes accessed | tf_op | source)
XLA Modules:
  0.0 277.5 jit_solution(8134928398966675628)
XLA Ops:
  1.3 273.5 %shard_map.77 = (bf16[64,192]{1,0:T(8,128)(2,1)}, bf16[2,64,128]{2,1,0:T(8,128)(2,1)}) custom-call(s32[1]{0:T(128)S(6)} %copy.10.t_ref, bf16[64,192]{1,0:T(8,128)(2,1)} %latent.1, bf16[3,8,3072]{2,1,0:T(8,128)(2,1)} %bitcast.16, bf16[3,4,4,192,128]{4,3,2,1,0:T(8,128)(2,1)} %bitcast.14, bf16[192,2048]{1,0:T(8,128)(2,1)} %bitcast.15, bf16[2,64,128]{2,1,0:T(8,128)(2,1)} %bitcast.17), custom_call_target="tpu_custom_call" | custom-call | tf_op jit(solution)/shard_map/pallas_call | solution.py:534
  274.7 1.4 copy.11
  276.1 1.4 copy.12

commit v4 on v3

--- a/solution.py
+++ b/solution.py
@@ -24,6 +24,7 @@
 FIRST = 5
 HOST = (0, 0, 0, 0, 0, 3, 0, 1, 2, 2, 3, 3, 0, 0, 1, 1)
 CHUNKS = 3 * YS + 1
+CROSS = 9
 
 
 def host_of(section):
@@ -40,7 +41,7 @@
     wbuf, wobuf, modbuf, vecs, cache, hb, hwide, att, own, wide, hst, hland, kvland, nrm,
     wot, base, shifted,
     ld_sem, h_send, h_recv, a_send, a_recv,
-    w_send, w_recv, f_send, f_recv, s_send, s_recv, o_send, o_recv,
+    w_send, w_recv, f_send, f_recv, m_send, m_recv, s_send, s_recv, o_send, o_recv,
 ):
     sec = lax.axis_index("section")
     me = lax.axis_index("seq")
@@ -51,6 +52,13 @@
     spread = sec < FIRST
     hosting = (sec >= FIRST) & (zh == place)
     helping = (sec >= FIRST) & (zh != place)
+    other = 1 - cfg
+    crossed = sec >= CROSS
+    branch = jnp.where(crossed, other, cfg)
+
+    def core_at(section):
+        return jnp.where(section >= CROSS, 1 - branch, branch)
+
 
     def rows(patch):
         return pl.ds(patch * PATCH_TOK, PATCH_TOK)
@@ -109,9 +117,14 @@
 
     @pl.when(jnp.logical_not(helping))
     def _():
-        for one in loads:
+        for one in loads[2:]:
             one.start()
 
+        @pl.when(jnp.logical_not(crossed))
+        def _():
+            for one in loads[:2]:
+                one.start()
+
     barrier = pltpu.get_barrier_semaphore()
 
     @pl.when(spread)
@@ -120,43 +133,50 @@
 
         @pl.when(sec > 0)
         def _():
-            loop(0, SEQ, lambda j: greet((sec - 1, j, cfg)))
+            loop(0, SEQ, lambda j: greet((sec - 1, j, core_at(sec - 1))))
+
+        greet((sec, me, other))
 
     @pl.when(hosting)
     def _():
-        each_helper(lambda z: greet((sec, z * YS + y, cfg)))
-        greet((sec, me, 1 - cfg))
+        def helper(z):
+            greet((sec, z * YS + y, cfg))
+            greet((sec, z * YS + y, other))
+
+        each_helper(helper)
+        greet((sec, me, other))
         each_ring(lambda col: greet((sec, place * YS + col, cfg)), False)
 
         @pl.when(sec == FIRST)
         def _():
-            loop(0, SEQ, lambda j: greet((sec - 1, j, cfg)))
+            loop(0, SEQ, lambda j: greet((sec - 1, j, core_at(sec - 1))))
 
         @pl.when(sec > FIRST)
         def _():
             before = host_of(sec - 1) * YS
-            loop(0, YS, lambda j: greet((sec - 1, before + j, cfg)))
+            loop(0, YS, lambda j: greet((sec - 1, before + j, core_at(sec - 1))))
 
     @pl.when(helping)
     def _():
         greet((sec, place * YS + y, cfg))
-        pl.semaphore_wait(barrier, 1)
+        greet((sec, place * YS + y, other))
+        pl.semaphore_wait(barrier, 2)
 
     @pl.when(sec < FIRST - 1)
     def _():
-        pl.semaphore_wait(barrier, SEQ - 1 + SEQ)
+        pl.semaphore_wait(barrier, SEQ + SEQ)
 
     @pl.when(sec == FIRST - 1)
     def _():
-        pl.semaphore_wait(barrier, SEQ - 1 + YS)
+        pl.semaphore_wait(barrier, SEQ + YS)
 
     @pl.when(hosting & (sec < LAYERS - 1))
     def _():
-        pl.semaphore_wait(barrier, 2 * YS - 1 + ZS)
+        pl.semaphore_wait(barrier, 2 * YS + 2 * (ZS - 1))
 
     @pl.when(hosting & (sec == LAYERS - 1))
     def _():
-        pl.semaphore_wait(barrier, YS - 1 + ZS)
+        pl.semaphore_wait(barrier, YS + 2 * (ZS - 1))
 
     def chunk_at(number, half, z):
         if number == CHUNKS - 1:
@@ -190,9 +210,12 @@
             spot, spot, f_send.at[z, number], f_recv.at[z, number], (sec, me, 1 - cfg)
         )
 
-    def s_copy():
-        return remote(
-            stale, cache.at[zh], s_send, s_recv.at[zh], (sec, place * YS + y, cfg)
+    def m_copy():
+        return remote(mod, modbuf, m_send, m_recv, (sec, me, other))
+
+    def s_copy(to, core):
+        return remote(
+            stale, cache.at[zh], s_send, s_recv.at[zh], (sec, to * YS + y, core)
         )
 
     def s_landing(z):
@@ -203,25 +226,48 @@
     def o_copy(z, number):
         src = cache.at[z] if number == 2 else hst.at[z, rows(number)]
         dst = kvland if number == 2 else hland.at[rows(number)]
-        return remote(src, dst, o_send.at[z, number], o_recv.at[number], (sec, z * YS + y, cfg))
+        return remote(
+            src, dst, o_send.at[z, number], o_recv.at[number], (sec, z * YS + y, branch)
+        )
+
+    def take_back():
+        for number in range(3):
+            o_copy(zh, number).wait_recv()
+        hid_out[...] = hland[...]
+        kv_out[...] = kvland[...]
 
     @pl.when(helping)
     def _():
-        s_copy().start()
+        s_copy(place, branch).start()
         for number in range(CHUNKS):
             w_copy(number).start()
         for number in range(CHUNKS):
             w_copy(number).wait_send()
-        s_copy().wait_send()
-        for number in range(3):
-            o_copy(zh, number).wait_recv()
-        hid_out[...] = hland[...]
-        kv_out[...] = kvland[...]
+        s_copy(place, branch).wait_send()
+        take_back()
+
+    @pl.when(jnp.logical_not(helping) & crossed)
+    def _():
+        m_copy().start()
+        s_copy(zh, other).start()
+
+    def own_arrays():
+        @pl.when(crossed)
+        def _():
+            m_copy().wait()
+            s_copy(zh, other).wait_send()
+            s_landing(zh).wait_recv()
+
+        @pl.when(jnp.logical_not(crossed))
+        def _():
+            loads[0].wait()
+            loads[1].wait()
 
     def h_copy(patch, section, to):
         return remote(
             own.at[rows(patch)], hb.at[patch, me],
-            h_send.at[patch, to], h_recv.at[patch, me], (section, to, cfg),
+            h_send.at[patch, to], h_recv.at[patch, me],
+            (section, to, core_at(section)),
         )
 
     def h_landing(patch, source):
@@ -233,7 +279,7 @@
     def wide_copy(patch, to, col):
         return remote(
             wide.at[patch], hwide.at[patch, y],
-            h_send.at[patch, col], h_recv.at[patch, y], (sec + 1, to * YS + col, cfg),
+            h_send.at[patch, col], h_recv.at[patch, y], (sec + 1, to * YS + col, core_at(sec + 1)),
         )
 
     def wide_landing(patch, col):
@@ -260,7 +306,7 @@
         return (values * (1.0 / jnp.sqrt(square + EPS_NORM))).astype(jnp.bfloat16)
 
     def modulation_rows():
-        loads[0].wait()
+        own_arrays()
         pick = lax.broadcasted_iota(jnp.int32, (8, D), 0) == t_ref[0]
         for part in range(3):
             row = jnp.sum(
@@ -323,10 +369,22 @@
             update = term if update is None else update + term
         return update
 
+    def finish(z):
+        @pl.when(crossed)
+        def _():
+            for number in range(3):
+                o_copy(z, number).start()
+            take_back()
+            for number in range(3):
+                o_copy(z, number).wait_send()
+
+        @pl.when(jnp.logical_not(crossed))
+        def _():
+            hid_out[...] = hst[z]
+            kv_out[...] = cache[z]
+
     @pl.when(spread)
     def _():
-        modulation_rows()
-        loads[1].wait()
         loads[2].wait()
 
         @pl.when(sec == 0)
@@ -334,6 +392,8 @@
             for patch in range(PATCHES):
                 each_peer(lambda to: h_copy(patch, sec, to).start(), False)
                 hb[patch, me] = own[rows(patch)]
+
+        modulation_rows()
 
         def front(patch):
             @pl.when(sec == 0)
@@ -384,13 +444,13 @@
                     lambda col: h_copy(patch, sec + 1, HOST[FIRST] * YS + col).start(), True
                 )
 
-            hid_out[rows(patch), :] = result
+            hst[zh, rows(patch), :] = result
 
         for patch in range(PATCHES):
             front(patch)
         for patch in range(PATCHES):
             back(patch)
-        kv_out[...] = cache[zh]
+        finish(zh)
         for patch in range(PATCHES):
             each_peer(lambda to: a_copy(patch, me, to).wait_send(), False)
 
@@ -407,7 +467,7 @@
     @pl.when(hosting)
     def _():
         modulation_rows()
-        for one in loads[1:]:
+        for one in loads[2:]:
             one.wait()
         for number in range(CHUNKS):
             def relay(z, number=number):
@@ -452,7 +512,7 @@
                 assemble(patch)
 
             total, parts = None, []
-            for dy in (0, 1, 3, 2):
+            for dy in (2, 3, 1, 0):
                 col = lax.rem(y + dy, YS)
 
                 @pl.when(sec > FIRST)
@@ -513,8 +573,7 @@
         each_helper(lambda z: o_copy(z, 2).start())
         for patch in range(PATCHES):
             back(patch)
-        kv_out[...] = cache[place]
-        hid_out[...] = hst[place]
+        finish(place)
         for patch in range(PATCHES):
             each_ring(lambda col: ring_copy(patch, y, col).wait_send(), False)
 
@@ -567,6 +626,8 @@
             dma((ZS, CHUNKS)),
             dma((ZS, CHUNKS)),
             dma,
+            dma,
+            dma,
             dma((ZS,)),
             dma((ZS, 3)),
             dma((3,)),

time: 278 us -> 265 us (0.953)
  Pallas kernels: 273 us -> 261 us
    pallas_call x1, Pallas kernels: 273 us -> 261 us  [on_device(): pl.pallas_call(kernel, out_shape=(jax.ShapeDtypeStruct((TOKENS, WIDTH), b...]
where the time goes in v4:
time: 265 us
  Pallas kernels  261 us (98%)
  local copies, waits for them, and re-layouts  2.75 us (1%)
    pallas_call x1, Pallas kernels, on_device(): pl.pallas_call(kernel, out_shape=(jax.ShapeDtypeStruct((TOKENS, WIDTH), b...  261 us

profile of v4, /device:TPU:102, one launch (start us, length us, event | category | flops | bytes accessed | tf_op | source)
XLA Modules:
  0.0 264.7 jit_solution(4216271278854553442)
XLA Ops:
  1.3 260.6 %shard_map.77 = (bf16[64,192]{1,0:T(8,128)(2,1)}, bf16[2,64,128]{2,1,0:T(8,128)(2,1)}) custom-call(s32[1]{0:T(128)S(6)} %copy.10.t_ref, bf16[64,192]{1,0:T(8,128)(2,1)} %latent.1, bf16[3,8,3072]{2,1,0:T(8,128)(2,1)} %bitcast.16, bf16[3,4,4,192,128]{4,3,2,1,0:T(8,128)(2,1)} %bitcast.14, bf16[192,2048]{1,0:T(8,128)(2,1)} %bitcast.15, bf16[2,64,128]{2,1,0:T(8,128)(2,1)} %bitcast.17), custom_call_target="tpu_custom_call" | custom-call | tf_op jit(solution)/shard_map/pallas_call | solution.py:593
  261.9 1.4 copy.11
  263.3 1.4 copy.12

commit v5 on v4

--- a/solution.py
+++ b/solution.py
@@ -24,7 +24,7 @@
 FIRST = 5
 HOST = (0, 0, 0, 0, 0, 3, 0, 1, 2, 2, 3, 3, 0, 0, 1, 1)
 CHUNKS = 3 * YS + 1
-CROSS = 9
+CROSS = 10
 
 
 def host_of(section):
@@ -38,7 +38,7 @@
 def kernel(
     t_ref, latent, mod, wq, wo, stale,
     hid_out, kv_out,
-    wbuf, wobuf, modbuf, vecs, cache, hb, hwide, att, own, wide, hst, hland, kvland, nrm,
+    wbuf, wobuf, modbuf, vecs, cache, hb, hwide, att, own, wide, hst, hland, kvland,
     wot, base, shifted,
     ld_sem, h_send, h_recv, a_send, a_recv,
     w_send, w_recv, f_send, f_recv, m_send, m_recv, s_send, s_recv, o_send, o_recv,
@@ -110,7 +110,7 @@
             loads.append(
                 pltpu.make_async_copy(
                     wq.at[part, :, col],
-                    wbuf.at[col, :, :, lanes(part * ZS + zh)],
+                    wbuf.at[part * ZS + zh, col],
                     ld_sem.at[4 + part * YS + col],
                 )
             )
@@ -184,7 +184,7 @@
                 pl.ds(pl.multiple_of(z * WIDTH, WIDTH), WIDTH), lanes(half, INNER // 2)
             ]
         part, col = divmod(number, YS)
-        return wbuf.at[col, pl.ds(half * 2, 2), :, lanes(part * ZS + z)]
+        return wbuf.at[part * ZS + z, col, pl.ds(half * 2, 2)]
 
     def chunk_from(number, half):
         if number == CHUNKS - 1:
@@ -295,7 +295,7 @@
         )
 
     def ring_copy(patch, source, to):
-        spot = att.at[patch, :, :, lanes(source)]
+        spot = att.at[patch, source]
         return remote(
             spot, spot, a_send.at[patch, to], a_recv.at[patch, source],
             (sec, place * YS + to, cfg),
@@ -305,21 +305,70 @@
         square = jnp.mean(values * values, axis=-1, keepdims=True)
         return (values * (1.0 / jnp.sqrt(square + EPS_NORM))).astype(jnp.bfloat16)
 
-    def modulation_rows():
+    def weights(col):
+        return jnp.concatenate(
+            [wbuf[number, col].reshape(WIDE, HEAD_DIM) for number in range(3 * ZS)], axis=1
+        )
+
+    def own_weights(z):
+        return jnp.concatenate(
+            [wbuf[part * ZS + zh, :, z].reshape(WIDE, HEAD_DIM) for part in range(3)], axis=1
+        )
+
+    def column_sums(weights_of):
+        which = lax.broadcasted_iota(jnp.int32, (16, WIDE), 0)
+        shift_sum = None
+        for number in range(YS):
+            here = slice(number * WIDE, (number + 1) * WIDE)
+            scale = vecs[1, :, here]
+            high = scale.astype(jnp.bfloat16).astype(jnp.float32)
+            stack = jnp.where(
+                which == 0, high,
+                jnp.where(which == 1, scale - high, jnp.where(which == 2, vecs[0, :, here], 0.0)),
+            )
+            sums = jnp.dot(
+                stack.astype(jnp.bfloat16), weights_of(number), preferred_element_type=jnp.float32
+            )
+            size = sums.shape[1]
+            base[number, :, :size] = sums[0:1] + sums[1:2]
+            shift_sum = sums[2:3] if shift_sum is None else shift_sum + sums[2:3]
+        shifted[:, :size] = shift_sum
+
+    def project(order, block_of, weights_of, size):
+        total, parts = None, []
+        for number in order:
+            block = block_of(number)
+            middle = jnp.mean(block, axis=-1, keepdims=True)
+            block = block - middle
+            parts.append((number, middle, jnp.sum(block * block, axis=-1, keepdims=True)))
+            term = jnp.dot(
+                (block * vecs[1, :, lanes(number, WIDE)]).astype(jnp.bfloat16),
+                weights_of(number),
+                preferred_element_type=jnp.float32,
+            )
+            total = term if total is None else total + term
+        mean = sum(part[1] for part in parts) * (1.0 / YS)
+        spread_of = sum(part[2] + WIDE * (part[1] - mean) ** 2 for part in parts) * (1.0 / D)
+        for number, middle, _ in parts:
+            total = total + (middle - mean) * base[number, :, :size]
+        return total * (1.0 / jnp.sqrt(spread_of + EPS_NORM)) + shifted[:, :size]
+
+    def modulation_rows(ring):
         own_arrays()
         pick = lax.broadcasted_iota(jnp.int32, (8, D), 0) == t_ref[0]
         for part in range(3):
             row = jnp.sum(
                 jnp.where(pick, modbuf[part].astype(jnp.float32), 0.0), axis=0, keepdims=True
             )
-            row = jnp.concatenate(
-                [
-                    row[:, (z * YS + col) * WIDTH : (z * YS + col + 1) * WIDTH]
-                    for col in range(YS)
-                    for z in range(ZS)
-                ],
-                axis=1,
-            )
+            if ring:
+                row = jnp.concatenate(
+                    [
+                        row[:, (z * YS + col) * WIDTH : (z * YS + col + 1) * WIDTH]
+                        for col in range(YS)
+                        for z in range(ZS)
+                    ],
+                    axis=1,
+                )
             vecs[part] = row + 1.0 if part == 1 else row
 
     def assemble(patch):
@@ -327,16 +376,6 @@
             hwide[patch, col] = jnp.concatenate(
                 [hb[patch, z * YS + col].astype(jnp.float32) for z in range(ZS)], axis=1
             ).astype(jnp.bfloat16)
-
-    def normalise(patch):
-        whole = jnp.concatenate(
-            [hwide[patch, col].astype(jnp.float32) for col in range(YS)], axis=1
-        )
-        centred = whole - jnp.mean(whole, axis=-1, keepdims=True)
-        spread_of = jnp.mean(centred * centred, axis=-1, keepdims=True)
-        nrm[...] = (
-            centred * (1.0 / jnp.sqrt(spread_of + EPS_NORM)) * vecs[1] + vecs[0]
-        ).astype(jnp.bfloat16)
 
     def attend(patch, heads):
         for z, _, key, value in heads:
@@ -359,16 +398,6 @@
         ]
         return [block.astype(jnp.bfloat16) for block in attended]
 
-    def project_out(patch, weight):
-        update = None
-        for z in range(ZS):
-            term = lax.dot_general(
-                att[patch, z], weight(z), (((1,), (1,)), ((), ())),
-                preferred_element_type=jnp.float32,
-            )
-            update = term if update is None else update + term
-        return update
-
     def finish(z):
         @pl.when(crossed)
         def _():
@@ -393,44 +422,58 @@
                 each_peer(lambda to: h_copy(patch, sec, to).start(), False)
                 hb[patch, me] = own[rows(patch)]
 
-        modulation_rows()
+        modulation_rows(False)
+        for one in loads[4:]:
+            one.wait()
+        column_sums(own_weights)
 
         def front(patch):
+            def block_of(z):
+                def arrived(col):
+                    @pl.when((sec > 0) | (z * YS + col != me))
+                    def _():
+                        h_landing(patch, z * YS + col).wait_recv()
+
+                loop(0, YS, arrived)
+                return jnp.concatenate(
+                    [hb[patch, z * YS + col].astype(jnp.float32) for col in range(YS)], axis=1
+                )
+
+            projected = project(
+                [lax.rem(zh + dz, ZS) for dz in (0, 1, 3, 2)], block_of, own_weights, 3 * HEAD_DIM
+            )
+            three = [projected[:, part * HEAD_DIM : (part + 1) * HEAD_DIM] for part in range(3)]
+            att[patch, zh, :, lanes(y)] = attend(patch, [(zh, *three)])[0]
+            each_peer(lambda to: a_copy(patch, me, to).start(), False)
+
             @pl.when(sec == 0)
             def _():
-                each_peer(lambda to: h_landing(patch, to).wait_recv(), False)
                 each_peer(lambda to: h_copy(patch, sec, to).wait_send(), False)
-
-            @pl.when(sec > 0)
-            def _():
-                each_peer(lambda to: h_landing(patch, to).wait_recv(), True)
-
-            assemble(patch)
-            normalise(patch)
-            if patch == 0:
-                for one in loads[4:]:
-                    one.wait()
-            projected = [
-                jnp.dot(
-                    nrm[...],
-                    wbuf[:, :, :, lanes(part * ZS + zh)].reshape(D, HEAD_DIM),
-                    preferred_element_type=jnp.float32,
-                )
-                for part in range(3)
-            ]
-            att[patch, zh, :, lanes(y)] = attend(patch, [(zh, *projected)])[0]
-            each_peer(lambda to: a_copy(patch, me, to).start(), False)
 
         def back(patch):
             if patch == 0:
                 loads[3].wait()
-            mine = vecs[2, :, lanes(y, WIDE)]
+            mine = vecs[2, :, lanes(zh, WIDE)]
             gate = jnp.zeros((1, WIDTH), jnp.float32)
-            for z in range(ZS):
-                gate = gate + jnp.where(zh == z, mine[:, z * WIDTH : (z + 1) * WIDTH], 0.0)
-            each_peer(lambda to: a_copy(patch, to, to).wait_recv(), False)
+            for col in range(YS):
+                gate = gate + jnp.where(y == col, mine[:, col * WIDTH : (col + 1) * WIDTH], 0.0)
             part = pl.ds(pl.multiple_of(zh * WIDTH, WIDTH), WIDTH)
-            update = project_out(patch, lambda z: wobuf[part, z * GROUP : (z + 1) * GROUP])
+            update = None
+            for dz in (0, 1, 3, 2):
+                z = lax.rem(zh + dz, ZS)
+                loop(
+                    0 if dz else 1,
+                    YS,
+                    lambda j, z=z: a_copy(
+                        patch, z * YS + lax.rem(y + j, YS), z * YS + lax.rem(y + j, YS)
+                    ).wait_recv(),
+                )
+                term = lax.dot_general(
+                    att[patch, z], wobuf[part, lanes(z, GROUP)],
+                    (((1,), (1,)), ((), ())),
+                    preferred_element_type=jnp.float32,
+                )
+                update = term if update is None else update + term
             result = (hb[patch, me].astype(jnp.float32) + gate * update).astype(jnp.bfloat16)
             own[rows(patch)] = result
 
@@ -466,7 +509,7 @@
 
     @pl.when(hosting)
     def _():
-        modulation_rows()
+        modulation_rows(True)
         for one in loads[2:]:
             one.wait()
         for number in range(CHUNKS):
@@ -483,27 +526,11 @@
 
         def turn(j):
             at = lanes(j)
-            wot[at, :] = wobuf[:, at].T
+            wot[lanes(lax.rem(j, YS) * ZS + j // YS), :] = wobuf[:, at].T
 
         loop(0, INNER // HEAD_DIM, turn)
 
-        which = lax.broadcasted_iota(jnp.int32, (16, WIDE), 0)
-        shift_sum = None
-        for col in range(YS):
-            here = slice(col * WIDE, (col + 1) * WIDE)
-            scale = vecs[1, :, here]
-            high = scale.astype(jnp.bfloat16).astype(jnp.float32)
-            stack = jnp.where(
-                which == 0, high,
-                jnp.where(which == 1, scale - high, jnp.where(which == 2, vecs[0, :, here], 0.0)),
-            )
-            sums = jnp.dot(
-                stack.astype(jnp.bfloat16), wbuf[col].reshape(WIDE, 3 * GROUP),
-                preferred_element_type=jnp.float32,
-            )
-            base[col] = sums[0:1] + sums[1:2]
-            shift_sum = sums[2:3] if shift_sum is None else shift_sum + sums[2:3]
-        shifted[...] = shift_sum
+        column_sums(weights)
 
         def front(patch):
             @pl.when(sec == FIRST)
@@ -511,29 +538,16 @@
                 loop(0, SEQ, lambda j: h_landing(patch, j).wait_recv())
                 assemble(patch)
 
-            total, parts = None, []
-            for dy in (2, 3, 1, 0):
-                col = lax.rem(y + dy, YS)
-
+            def block_of(col):
                 @pl.when(sec > FIRST)
-                def _(col=col):
+                def _():
                     wide_landing(patch, col).wait_recv()
 
-                block = hwide[patch, col].astype(jnp.float32)
-                middle = jnp.mean(block, axis=-1, keepdims=True)
-                block = block - middle
-                parts.append((col, middle, jnp.sum(block * block, axis=-1, keepdims=True)))
-                term = jnp.dot(
-                    (block * vecs[1, :, lanes(col, WIDE)]).astype(jnp.bfloat16),
-                    wbuf[col].reshape(WIDE, 3 * GROUP),
-                    preferred_element_type=jnp.float32,
-                )
-                total = term if total is None else total + term
-            mean = sum(part[1] for part in parts) * (1.0 / YS)
-            spread_of = sum(part[2] + WIDE * (part[1] - mean) ** 2 for part in parts) * (1.0 / D)
-            for col, middle, _ in parts:
-                total = total + (middle - mean) * base[col]
-            projected = total * (1.0 / jnp.sqrt(spread_of + EPS_NORM)) + shifted[...]
+                return hwide[patch, col].astype(jnp.float32)
+
+            projected = project(
+                [lax.rem(y + dy, YS) for dy in (2, 3, 1, 0)], block_of, weights, 3 * GROUP
+            )
             attended = attend(
                 patch,
                 [
@@ -544,16 +558,17 @@
                     for z in range(ZS)
                 ],
             )
-            for z in range(ZS):
-                att[patch, z, :, lanes(y)] = attended[z]
+            att[patch, y] = jnp.concatenate(attended, axis=1)
             each_ring(lambda col: ring_copy(patch, y, col).start(), False)
 
         def back(patch):
-            each_ring(lambda col: ring_copy(patch, col, col).wait_recv(), False)
             update = None
-            for z in range(ZS):
+            for dy in (0, 3, 1, 2):
+                col = lax.rem(y + dy, YS)
+                if dy:
+                    ring_copy(patch, col, col).wait_recv()
                 term = jnp.dot(
-                    att[patch, z], wot[z * GROUP : (z + 1) * GROUP],
+                    att[patch, col], wot[lanes(col, GROUP), :],
                     preferred_element_type=jnp.float32,
                 )
                 update = term if update is None else update + term
@@ -566,14 +581,20 @@
 
             for z in range(ZS):
                 hst[z, rows(patch)] = result[:, z * WIDTH : (z + 1) * WIDTH].astype(jnp.bfloat16)
-            each_helper(lambda z: o_copy(z, patch).start())
+
+            @pl.when(sec == LAYERS - 1)
+            def _():
+                each_helper(lambda z: o_copy(z, patch).start())
 
         for patch in range(PATCHES):
             front(patch)
-        each_helper(lambda z: o_copy(z, 2).start())
+
+        @pl.when(sec == LAYERS - 1)
+        def _():
+            each_helper(lambda z: o_copy(z, 2).start())
+
         for patch in range(PATCHES):
             back(patch)
-        finish(place)
         for patch in range(PATCHES):
             each_ring(lambda col: ring_copy(patch, y, col).wait_send(), False)
 
@@ -581,8 +602,14 @@
             def _():
                 each_ring(lambda col: wide_copy(patch, after, col).wait_send(), True)
 
+        @pl.when(sec < LAYERS - 1)
+        def _():
+            for number in range(3):
+                each_helper(lambda z: o_copy(z, number).start())
+
         for number in range(3):
             each_helper(lambda z: o_copy(z, number).wait_send())
+        finish(place)
 
 
 def on_device(latent, timestep, modulation, qkv_weight, out_weight, stale_kv):
@@ -599,7 +626,7 @@
         in_specs=[pl.BlockSpec(memory_space=pltpu.SMEM)] + [any_space] * 5,
         out_specs=(in_vmem, in_vmem),
         scratch_shapes=[
-            pltpu.VMEM((YS, ZS, WIDTH, 3 * GROUP), bf16),
+            pltpu.VMEM((3 * ZS, YS, ZS, WIDTH, HEAD_DIM), bf16),
             pltpu.VMEM((WIDE, INNER), bf16),
             pltpu.VMEM((3, 8, D), bf16),
             pltpu.VMEM((3, 1, D), jnp.float32),
@@ -612,7 +639,6 @@
             pltpu.VMEM((ZS, TOKENS, WIDTH), bf16),
             pltpu.VMEM((TOKENS, WIDTH), bf16),
             pltpu.VMEM((2, TOKENS, HEAD_DIM), bf16),
-            pltpu.VMEM((PATCH_TOK, D), bf16),
             pltpu.VMEM((INNER, WIDE), bf16),
             pltpu.VMEM((YS, 1, 3 * GROUP), jnp.float32),
             pltpu.VMEM((1, 3 * GROUP), jnp.float32),

time: 265 us -> 261 us (0.985)
  Pallas kernels: 261 us -> 257 us
    pallas_call x1, Pallas kernels: 261 us -> 257 us  [on_device(): pl.pallas_call(kernel, out_shape=(jax.ShapeDtypeStruct((TOKENS, WIDTH), b...]
where the time goes in v5:
time: 261 us
  Pallas kernels  257 us (98%)
  local copies, waits for them, and re-layouts  2.75 us (1%)
    pallas_call x1, Pallas kernels, on_device(): pl.pallas_call(kernel, out_shape=(jax.ShapeDtypeStruct((TOKENS, WIDTH), b...  257 us

profile of v5, /device:TPU:102, one launch (start us, length us, event | category | flops | bytes accessed | tf_op | source)
XLA Modules:
  0.0 261.1 jit_solution(9467680607816066812)
XLA Ops:
  1.3 257.1 %shard_map.77 = (bf16[64,192]{1,0:T(8,128)(2,1)}, bf16[2,64,128]{2,1,0:T(8,128)(2,1)}) custom-call(s32[1]{0:T(128)S(6)} %copy.10.t_ref, bf16[64,192]{1,0:T(8,128)(2,1)} %latent.1, bf16[3,8,3072]{2,1,0:T(8,128)(2,1)} %bitcast.16, bf16[3,4,4,192,128]{4,3,2,1,0:T(8,128)(2,1)} %bitcast.14, bf16[192,2048]{1,0:T(8,128)(2,1)} %bitcast.15, bf16[2,64,128]{2,1,0:T(8,128)(2,1)} %bitcast.17), custom_call_target="tpu_custom_call" | custom-call | tf_op jit(solution)/shard_map/pallas_call | solution.py:620
  258.4 1.4 copy.11
  259.8 1.4 copy.12

commit v6 on v5

--- a/solution.py
+++ b/solution.py
@@ -91,7 +91,7 @@
             )
 
     def each_ring(act, with_self):
-        for dy in (2, 1, 3, 0) if with_self else (2, 1, 3):
+        for dy in (2, 1, 3, 0) if with_self else (1, 3, 2):
             act(lax.rem(y + dy, YS))
 
     def each_helper(act):

time: 261 us -> 260 us (level)
  no operation moved by 1% of the time
where the time goes in v6:
time: 260 us
  Pallas kernels  256 us (98%)
  local copies, waits for them, and re-layouts  2.75 us (1%)
    pallas_call x1, Pallas kernels, on_device(): pl.pallas_call(kernel, out_shape=(jax.ShapeDtypeStruct((TOKENS, WIDTH), b...  256 us

profile of v6, /device:TPU:102, one launch (start us, length us, event | category | flops | bytes accessed | tf_op | source)
XLA Modules:
  0.0 260.1 jit_solution(5185275605908438324)
XLA Ops:
  1.3 256.1 %shard_map.77 = (bf16[64,192]{1,0:T(8,128)(2,1)}, bf16[2,64,128]{2,1,0:T(8,128)(2,1)}) custom-call(s32[1]{0:T(128)S(6)} %copy.10.t_ref, bf16[64,192]{1,0:T(8,128)(2,1)} %latent.1, bf16[3,8,3072]{2,1,0:T(8,128)(2,1)} %bitcast.16, bf16[3,4,4,192,128]{4,3,2,1,0:T(8,128)(2,1)} %bitcast.14, bf16[192,2048]{1,0:T(8,128)(2,1)} %bitcast.15, bf16[2,64,128]{2,1,0:T(8,128)(2,1)} %bitcast.17), custom_call_target="tpu_custom_call" | custom-call | tf_op jit(solution)/shard_map/pallas_call | solution.py:620
  257.4 1.4 copy.11
  258.7 1.4 copy.12

commit v7 on v6

--- a/solution.py
+++ b/solution.py
@@ -584,14 +584,16 @@
 
             @pl.when(sec == LAYERS - 1)
             def _():
-                each_helper(lambda z: o_copy(z, patch).start())
+                for dz in (2, 1, 3):
+                    o_copy(lax.rem(place + dz, ZS), patch).start()
 
         for patch in range(PATCHES):
             front(patch)
 
         @pl.when(sec == LAYERS - 1)
         def _():
-            each_helper(lambda z: o_copy(z, 2).start())
+            for dz in (2, 1, 3):
+                o_copy(lax.rem(place + dz, ZS), 2).start()
 
         for patch in range(PATCHES):
             back(patch)

time: 260 us -> 261 us (level)
  no operation moved by 1% of the time
where the time goes in v7:
time: 261 us; the launch traced here: 260 us
  Pallas kernels  256 us (98%)
  local copies, waits for them, and re-layouts  2.75 us (1%)
    pallas_call x1, Pallas kernels, on_device(): pl.pallas_call(kernel, out_shape=(jax.ShapeDtypeStruct((TOKENS, WIDTH), b...  256 us

profile of v7, /device:TPU:102, one launch (start us, length us, event | category | flops | bytes accessed | tf_op | source)
XLA Modules:
  0.0 260.5 jit_solution(16805657377069527389)
XLA Ops:
  1.3 256.5 %shard_map.77 = (bf16[64,192]{1,0:T(8,128)(2,1)}, bf16[2,64,128]{2,1,0:T(8,128)(2,1)}) custom-call(s32[1]{0:T(128)S(6)} %copy.10.t_ref, bf16[64,192]{1,0:T(8,128)(2,1)} %latent.1, bf16[3,8,3072]{2,1,0:T(8,128)(2,1)} %bitcast.16, bf16[3,4,4,192,128]{4,3,2,1,0:T(8,128)(2,1)} %bitcast.14, bf16[192,2048]{1,0:T(8,128)(2,1)} %bitcast.15, bf16[2,64,128]{2,1,0:T(8,128)(2,1)} %bitcast.17), custom_call_target="tpu_custom_call" | custom-call | tf_op jit(solution)/shard_map/pallas_call | solution.py:622
  257.7 1.4 copy.11
  259.1 1.4 copy.12
